TPU v7x, 32 devices: a whole 2x2x4 slice. The times are simulated.
32 devices in a mesh: fsdp: 16 (over z, y, x), tensor: 2 (over core).
Axes of the slice: x: 2, y: 2, z: 4, core: 2. Of those that a mesh axis runs over, the one named last changes fastest.
Arguments:
- attention_output: bfloat16 [8192, 8192], P('fsdp', 'tensor'), may hold values from -6 to 6
- frozen_weight: bfloat16 [8192, 4096], P('tensor', 'fsdp'), may hold values from -0.397747564 to 0.397747564
- adapter_down: bfloat16 [8192, 64], P('tensor'), may hold values from -0.06629126 to 0.06629126
- adapter_up: bfloat16 [64, 4096], replicated, may hold values from -0.25 to 0.25
- magnitude: float32 [4096], replicated, may hold values from 0.25 to 1
- cotangent: bfloat16 [8192, 4096], P('fsdp', 'tensor'), may hold values from -3 to 3
Outputs:
- layer_out: bfloat16 [8192, 4096], P('fsdp', 'tensor')
- input_gradient: bfloat16 [8192, 8192], P('fsdp', 'tensor')
- down_gradient: float32 [8192, 64], P('tensor')
- d_up: float32 [64, 4096], P(None, 'tensor')
- d_magnitude: float32 [4096], P('tensor')
All inputs are finite; a program needn't handle non-finite values.
Results may differ from a plain program's by a relative error of at most 0.0085.
Values may be sent and summed in bfloat16 or wider, within the bound.
No kernel may reach another device: no remote copies, remote signals or barrier semaphores. Data moves between devices by JAX's collectives and lax.ppermute only.
A program may use at most 192 MiB of HBM per device.

v0:
```python
import jax
import jax.numpy as jnp
from jax import lax
from jax.sharding import PartitionSpec as P

eps_norm = 1e-06


def on_device(attention_output, frozen_weight, adapter_down, adapter_up, magnitude, cotangent):
    tensor_count = lax.axis_size("tensor")
    tensor_index = lax.axis_index("tensor")
    tok_rows = attention_output.shape[0]
    output_columns = adapter_up.shape[1]
    block_columns = output_columns // tensor_count
    grad_scale = (tok_rows * lax.axis_size("fsdp")) ** (-0.5)
    up_factor_single = adapter_up.astype(jnp.float32)
    down_gram_matrix = jnp.dot(adapter_down.T, adapter_down, preferred_element_type=jnp.float32)
    rank_all = jnp.dot(down_gram_matrix, up_factor_single, precision=lax.Precision.HIGHEST)
    lowrank_partial = jnp.dot(attention_output, adapter_down, preferred_element_type=jnp.float32)
    piece_columns = lax.all_gather(frozen_weight, "fsdp", axis=1, tiled=True)
    up_factor_block = adapter_up
    cross_term_block = jnp.dot(adapter_down.T, piece_columns, preferred_element_type=jnp.float32)
    product = jnp.dot(attention_output, piece_columns, preferred_element_type=jnp.float32)
    merged_weight = piece_columns.astype(jnp.float32) + jnp.dot(
        adapter_down, up_factor_block, preferred_element_type=jnp.float32
    )
    col_sq = jnp.sum(merged_weight * merged_weight, axis=0)
    squares = col_sq
    cross_term = cross_term_block
    product, squares, cross_term = (product, squares, cross_term)
    low_sum, square_sum = lax.psum((lowrank_partial, squares), "tensor")
    adapter_hidden = low_sum.astype(jnp.bfloat16)
    col_norms = jnp.sqrt(square_sum + eps_norm)
    col_scale = magnitude / col_norms
    project_block = lax.psum_scatter(
        cross_term + rank_all, "tensor", scatter_dimension=1, tiled=True
    )
    gathered_cot = lax.all_gather(cotangent, "tensor", axis=1, tiled=True)
    prescale_gradient = (gathered_cot.astype(jnp.float32) * col_scale[None, :]).astype(jnp.bfloat16)
    lowrank_gradient = jnp.dot(
        prescale_gradient, adapter_up.T, preferred_element_type=jnp.float32
    ).astype(jnp.bfloat16)
    in_term = jnp.dot(attention_output.T, lowrank_gradient, preferred_element_type=jnp.float32)
    block_offset = tensor_index * block_columns
    scale_block = lax.dynamic_slice_in_dim(col_scale, block_offset, block_columns, 0)
    norms_block = lax.dynamic_slice_in_dim(col_norms, block_offset, block_columns, 0)
    magnitude_block = lax.dynamic_slice_in_dim(magnitude, block_offset, block_columns, 0)
    grad_block = lax.dynamic_slice_in_dim(prescale_gradient, block_offset, block_columns, 1)
    up_term = jnp.dot(adapter_hidden.T, grad_block, preferred_element_type=jnp.float32)
    base_block = lax.psum_scatter(
        product.astype(jnp.bfloat16), "tensor", scatter_dimension=1, tiled=True
    ).astype(jnp.float32)
    up_factor_block = lax.dynamic_slice_in_dim(adapter_up, block_offset, block_columns, 1)
    pre_block = base_block + jnp.dot(
        adapter_hidden, up_factor_block, preferred_element_type=jnp.float32
    )
    weighted_local = jnp.sum(cotangent.astype(jnp.float32) * pre_block, axis=0) / norms_block
    weighted_block, in_sum, up_sum = lax.psum((weighted_local, in_term, up_term), "fsdp")
    coef_block = -weighted_block * magnitude_block / (norms_block * norms_block)
    column_coefficient = lax.all_gather(coef_block, "tensor", axis=0, tiled=True)
    layer_out = (pre_block * scale_block[None, :]).astype(jnp.bfloat16)
    scaled_up_factor = (column_coefficient[:, None] * up_factor_single.T).astype(jnp.bfloat16)
    up_inner_product = jnp.dot(adapter_up, scaled_up_factor, preferred_element_type=jnp.float32)
    piece_columns = lax.all_gather(frozen_weight, "fsdp", axis=1, tiled=True)
    gradient_running = lax.dot_general(
        prescale_gradient,
        piece_columns,
        (((1,), (1,)), ((), ())),
        preferred_element_type=jnp.float32,
    )
    norm_down = jnp.dot(piece_columns, scaled_up_factor, preferred_element_type=jnp.float32)
    gradient_running, norm_down = (gradient_running, norm_down)
    input_gradient = (
        gradient_running
        + jnp.dot(lowrank_gradient, adapter_down.T, preferred_element_type=jnp.float32)
    ).astype(jnp.bfloat16)
    down_gradient = (
        in_sum
        + norm_down
        + jnp.dot(
            adapter_down.astype(jnp.float32), up_inner_product, precision=lax.Precision.HIGHEST
        )
    ) * grad_scale
    d_up = (up_sum + project_block * coef_block[None, :]) * grad_scale
    d_magnitude = weighted_block * grad_scale
    return (layer_out, input_gradient, down_gradient, d_up, d_magnitude)


def solution(mesh):
    return jax.shard_map(
        on_device,
        mesh=mesh,
        in_specs=(
            P("fsdp", "tensor"),
            P("tensor", "fsdp"),
            P("tensor", None),
            P(),
            P(),
            P("fsdp", "tensor"),
        ),
        out_specs=(
            P("fsdp", "tensor"),
            P("fsdp", "tensor"),
            P("tensor", None),
            P(None, "tensor"),
            P("tensor"),
        ),
        check_vma=False,
    )
```

profile of v0, /device:TPU:0, one launch (start us, length us, event | category | flops | bytes accessed | tf_op | source)
XLA Modules:
  0.0 898.4 jit_solution(15525175824476734400)
XLA Ops:
  7.2 0.0 copy-start
  7.2 0.0 all-gather.3.cloned.1.call-start
  7.2 0.7 all-gather.3.cloned.1.call-update
  7.9 0.0 all-gather.5.cloned.1.call-start
  8.0 0.7 all-gather.5.cloned.1.call-update
  8.7 0.0 reduce-scatter.3.cloned.1.call-start
  8.7 687.5 %all-gather.3.cloned.1.call-done = bf16[4096,4096]{1,0:T(8,128)(2,1)} async-done(((bf16[4096,256]{1,0:T(8,128)(2,1)}), bf16[4096,4096]{1,0:T(8,128)(2,1)}) %all-gather.3.cloned.1.call-update) | async-done | bytes 33554448 | tf_op jit(solution)/shard_map/all_gather | solution.py:20
  696.2 23.9 %convolution_convert_fusion = bf16[512,4096]{1,0:T(8,128)(2,1)} fusion(bf16[512,4096]{1,0:T(8,128)(2,1)} %param.6, bf16[4096,4096]{1,0:T(8,128)(2,1)} %all-gather.3.cloned.1.call-done), kind=kOutput, calls=%fused_computation.3 | convolution fusion | flops 17181966336 | bytes 41943040 | tf_op jit(solution)/shard_map/dot_general | solution.py:23
  720.1 0.0 copy-start.3
  720.1 0.0 reduce-scatter.3.cloned.1.call-update
  720.1 0.0 all-reduce.5.cloned.1.call-start
  720.2 0.0 copy-done
  720.2 3.6 fusion.14
  723.8 0.3 fusion.17
  724.1 0.0 copy-done.3
  724.1 0.0 copy-start.6
  724.1 15.4 %multiply_reduce_fusion = f32[4096]{0:T(1024)S(1)} fusion(bf16[4096,4096]{1,0:T(8,128)(2,1)} %all-gather.3.cloned.1.call-done, bf16[4096,64]{0,1:T(8,128)(2,1)S(1)} %copy-done, bf16[64,4096]{1,0:T(8,128)(2,1)S(1)} %copy-done.3), kind=kOutput, calls=%fused_computation | convolution fusion | flops 2214588416 | bytes 34619392 | tf_op jit(solution)/shard_map/dot_general | solution.py:24
  739.6 3.9 all-reduce.6
  743.4 0.0 copy-done.6
  743.5 0.0 all-gather.5.cloned.1.call-done
  743.5 3.0 multiply_convert_fusion
  746.6 0.0 copy-start.1
  746.6 0.0 copy-start.2
  746.6 1.3 fusion.3
  747.9 1.1 copy-done.1
  749.0 1.4 convolution_convert_fusion.1
  750.3 0.1 copy-done.2
  750.5 1.8 convolution_bitcast_fusion.1
  752.3 0.0 all-reduce.5.cloned.1.call-update
  752.3 0.2 reduce-scatter.5.cloned.1.call-start
  752.6 24.0 %fusion.15 = f32[512,4096]{1,0:T(8,128)} fusion(bf16[512,4096]{1,0:T(8,128)(2,1)} %copy-done.1, bf16[4096,4096]{1,0:T(8,128)(2,1)} %all-gather.3.cloned.1.call-done), kind=kOutput, calls=%fused_computation.33 | convolution fusion | flops 17179869184 | bytes 46137344 | tf_op jit(solution)/shard_map/dot_general | solution.py:65
  776.6 13.8 %fusion.16 = f32[64,4096]{1,0:T(8,128)S(1)} fusion(bf16[4096,64]{0,1:T(8,128)(2,1)S(1)} %copy-done, bf16[4096,4096]{1,0:T(8,128)(2,1)} %all-gather.3.cloned.1.call-done), kind=kOutput, calls=%fused_computation.34 | convolution fusion | flops 2147483648 | bytes 35127296 | tf_op jit(solution)/shard_map/dot_general | solution.py:22
  790.4 1.6 convolution_add_fusion
  792.0 0.0 copy-start.4
  792.0 6.8 add_convert_fusion
  798.8 0.0 reduce-scatter.5.cloned.1.call-update
  798.8 0.0 reduce-scatter.3.cloned.1.call-done
  798.9 0.0 copy-done.4
  798.9 4.1 multiply_reduce_fusion.1
  802.9 40.7 %psum.38 = f32[2048]{0:T(1024)S(1)} all-reduce(f32[2048]{0:T(1024)S(1)} %dynamic-slice_divide_fusion), channel_id=1, replica_groups=mesh['fsdp'=16,'tensor'=2] {'fsdp'}, use_global_device_ids=true, to_apply=%region_6.0 | all-reduce | flops 2048 | bytes 16384 | tf_op jit(solution)/shard_map/psum | solution.py:58
  843.6 0.6 broadcast_multiply_fusion
  844.2 1.8 all_gather.12
  846.0 0.3 fusion.5
  846.3 25.9 %all-reduce.5.cloned.1.call-done = (f32[4096,64]{0,1:T(8,128)}, f32[64,2048]{1,0:T(8,128)}) async-done(((f32[4096,64]{0,1:T(8,128)}, f32[64,2048]{1,0:T(8,128)}), (f32[4096,64]{0,1:T(8,128)}, f32[64,2048]{1,0:T(8,128)})) %all-reduce.5.cloned.1.call-update) | async-done | bytes 1572880 | tf_op jit(solution)/shard_map/psum | solution.py:58
  872.3 16.1 %fusion.2 = f32[4096,64]{0,1:T(8,128)S(1)} fusion(f32[4096,64]{0,1:T(8,128)} %get-tuple-element.5, bf16[4096,4096]{1,0:T(8,128)(2,1)} %all-gather.3.cloned.1.call-done, bf16[64,4096]{1,0:T(8,128)(2,1)S(1)} %copy-done.3, f32[4096]{0:T(1024)S(1)} %all_gather.12), kind=kOutput, calls=%fused_computation.10 | convolution fusion | flops 2148532224 | bytes 36192256 | tf_op jit(solution)/shard_map/dot_general | solution.py:71
  888.4 1.6 fusion.1
  890.0 0.0 copy-done.5
  890.0 1.9 add_multiply_fusion
  (5 shorter events, 0.0 us)
Async XLA Ops:
  7.2 713.0 %copy-start = (bf16[4096,64]{0,1:T(8,128)(2,1)S(1)}, bf16[4096,64]{0,1:T(8,128)(2,1)}, u32[]{:S(2)}) copy-start(bf16[4096,64]{0,1:T(8,128)(2,1)} %param.8) | copy-start | bytes 1572868
  7.2 689.0 %all-gather.3.cloned.1.call-start = ((), (), s32[]{:S(2)}) async-start(), calls=%async_computation.2 | async-start | bytes 35651584 | tf_op jit(solution)/shard_map/all_gather | solution.py:20
  7.9 735.6 %all-gather.5.cloned.1.call-start = ((), (), s32[]{:S(2)}) async-start(), calls=%async_computation.4 | async-start | bytes 6291456 | tf_op jit(solution)/shard_map/all_gather | solution.py:38
  8.7 790.2 %reduce-scatter.3.cloned.1.call-start = ((), (), s32[]{:S(2)}) async-start(), calls=%async_computation.3 | async-start | bytes 6291456 | tf_op jit(solution)/shard_map/reduce_scatter | solution.py:50
  720.1 4.0 copy-start.3
  720.1 152.2 %all-reduce.5.cloned.1.call-start = ((), (), s32[]{:S(2)}) async-start(), calls=%async_computation.6 | async-start | bytes 3145728 | tf_op jit(solution)/shard_map/psum | solution.py:58
  724.1 19.3 %copy-start.6 = (f32[4096]{0:T(1024)S(1)}, f32[4096]{0:T(1024)}, u32[]{:S(2)}) copy-start(f32[4096]{0:T(1024)} %param.10) | copy-start | bytes 49156
  746.6 2.4 copy-start.1
  746.6 3.9 copy-start.2
  752.3 137.7 %reduce-scatter.5.cloned.1.call-start = ((), (), s32[]{:S(2)}) async-start(), calls=%async_computation.5 | async-start | bytes 1572864 | tf_op jit(solution)/shard_map/reduce_scatter | solution.py:35
  792.0 6.9 copy-start.4
  872.3 17.7 %copy-start.5 = (f32[64,2048]{1,0:T(8,128)S(1)}, f32[64,2048]{1,0:T(8,128)}, u32[]{:S(2)}) copy-start(f32[64,2048]{1,0:T(8,128)} %get-tuple-element.6) | copy-start | bytes 1572868
Sparse Core Ops, SparseCore 0:
  9.5 686.6 all-gather.2
  697.8 14.8 all-gather.4
  720.2 13.5 reduce-scatter.2
  752.4 119.7 all-reduce.4
  874.4 7.7 reduce-scatter.4
where the time goes:
time: 899 us; the launch traced here: 898 us
  waiting for transfers between devices  715 us (80%)
  matrix products  116 us (13%)
  blocking collectives  46.4 us (5%)
  between operations  13.9 us (2%)
    all_gather x1, waiting for transfers between devices, on_device(): piece_columns = lax.all_gather(frozen_weight, 'fsdp', axis=1, tiled=True)  688 us
    psum x1, blocking collectives, on_device(): lax.psum((weighted_local, in_term, up_term), 'fsdp')  40.7 us
    psum x1, waiting for transfers between devices, on_device(): lax.psum((weighted_local, in_term, up_term), 'fsdp')  25.9 us
    dot_general x1, matrix products, on_device(): lax.dot_general(prescale_gradient, piece_columns, (((1,), (1,)), ((), ())...  24 us
    dot_general x1, matrix products, on_device(): jnp.dot(attention_output, piece_columns, preferred_element_type=jnp.float32)  23.9 us
  transfers between devices with their start and end apart: 5, of which 2 were waited for; matrix products, arithmetic and copies ran while one was open for 13% of the time, Pallas kernels for 0%

commit v1 on v0

v1 whole, which is shorter than its diff:
```python
import jax
import jax.numpy as jnp
from jax import lax
from jax.sharding import PartitionSpec as P

eps_norm = 1e-06
routes = ("xzy", "yzx", "zxy", "zyx")


def flip(value, axis, bit):
    pairs = [(i, i ^ bit) for i in range(lax.axis_size(axis))]
    return lax.ppermute(value, axis, pairs)


def sum_over(value, axis):
    bit = 1
    while bit < lax.axis_size(axis):
        value = value + flip(value, axis, bit)
        bit *= 2
    return value


def arrivals(z, depth):
    found = [("own", 0)]
    for hops in range(1, depth):
        if z - hops >= 0:
            found.append(("up", hops))
        if z + hops < depth:
            found.append(("down", hops))
    return found


def source_plane(z, depth):
    return [z - hops if way == "up" else z + hops for way, hops in arrivals(z, depth)]


def along_z(block, z, depth):
    count = 4 * depth
    held = {("own", 0): block}
    up = down = block
    for hops in range(1, depth):
        up = lax.ppermute(up, "fsdp", [(i, i + 4) for i in range(count - 4) if i // 4 >= hops - 1])
        down = lax.ppermute(
            down, "fsdp", [(i, i - 4) for i in range(4, count) if i // 4 + hops - 1 < depth]
        )
        held["up", hops] = up
        held["down", hops] = down
    placed = []
    for position in range(depth):
        wanted = [arrivals(plane, depth)[position] for plane in range(depth)]
        chosen = held[wanted[0]]
        for source in sorted(set(wanted) - {wanted[0]}):
            here = sum((z == plane) for plane in range(depth) if wanted[plane] == source) > 0
            chosen = jnp.where(here, held[source], chosen)
        placed.append(chosen)
    return placed


def both(block, place, bit, axis):
    other = flip(block, "fsdp", bit)
    low = jnp.where(place == 0, block, other)
    high = jnp.where(place == 0, other, block)
    return jnp.stack([low, high], axis=axis)


def gather_planes(piece, route, x, y, z, depth):
    def in_plane(block, way):
        if way == "x":
            return both(block, x, 1, block.ndim - 2)
        return both(block, y, 2, 0)

    blocks = [piece]
    for way in route:
        if way == "z":
            blocks = along_z(blocks[0], z, depth)
        else:
            blocks = [in_plane(block, way) for block in blocks]
    return [block.reshape(-1, piece.shape[-1]) for block in blocks]


def nt(a, b):
    return lax.dot_general(a, b, (((1,), (1,)), ((), ())), preferred_element_type=jnp.float32)


def nn(a, b):
    return jnp.dot(a, b, preferred_element_type=jnp.float32)


def tn(a, b):
    return lax.dot_general(a, b, (((0,), (0,)), ((), ())), preferred_element_type=jnp.float32)


def on_device(attention_output, frozen_weight, adapter_down, adapter_up, magnitude, cotangent):
    tensor_count = lax.axis_size("tensor")
    tensor_index = lax.axis_index("tensor")
    fsdp_count = lax.axis_size("fsdp")
    fsdp_index = lax.axis_index("fsdp")
    depth = fsdp_count // 4
    x, y, z = fsdp_index % 2, (fsdp_index // 2) % 2, fsdp_index // 4
    tok_rows, in_rows = attention_output.shape
    rank, output_columns = adapter_up.shape
    own_columns = frozen_weight.shape[1]
    block_columns = output_columns // tensor_count
    plane_columns = output_columns // depth
    block_planes = depth // tensor_count
    grad_scale = (tok_rows * fsdp_count) ** (-0.5)

    weight_t = frozen_weight.T
    step = in_rows // len(routes)
    cuts = [(i * step, (i + 1) * step) for i in range(len(routes))]
    gathered = [
        gather_planes(weight_t[:, low:high], route, x, y, z, depth)
        for (low, high), route in zip(cuts, routes)
    ]
    planes = jnp.array([source_plane(i, depth) for i in range(depth)], jnp.int32)
    plane_of = lax.dynamic_index_in_dim(planes, z, 0, keepdims=False)
    positions = jnp.array(
        [[source_plane(i, depth).index(p) for p in range(depth)] for i in range(depth)], jnp.int32
    )
    position_of = lax.dynamic_index_in_dim(positions, z, 0, keepdims=False)

    up_own = lax.dynamic_slice_in_dim(adapter_up, fsdp_index * own_columns, own_columns, 1)
    merged = frozen_weight.astype(jnp.float32) + nn(adapter_down, up_own)
    square_own = sum_over(jnp.sum(merged * merged, axis=0), "tensor")
    square_sum = lax.all_gather(square_own, "fsdp", axis=0, tiled=True)
    col_norms = jnp.sqrt(square_sum + eps_norm)
    col_scale = magnitude / col_norms

    adapter_hidden = sum_over(nn(attention_output, adapter_down), "tensor").astype(jnp.bfloat16)

    gathered_cot = lax.all_gather(cotangent, "tensor", axis=1, tiled=True)
    prescale_gradient = (gathered_cot.astype(jnp.float32) * col_scale[None, :]).astype(jnp.bfloat16)
    lowrank_gradient = nt(prescale_gradient, adapter_up).astype(jnp.bfloat16)
    in_term = tn(attention_output, lowrank_gradient)
    block_offset = tensor_index * block_columns

    def own_block(vector):
        return lax.dynamic_slice_in_dim(vector, block_offset, block_columns, vector.ndim - 1)

    scale_block = own_block(col_scale)
    norms_block = own_block(col_norms)
    magnitude_block = own_block(magnitude)
    grad_block = (cotangent.astype(jnp.float32) * scale_block[None, :]).astype(jnp.bfloat16)
    up_term = tn(adapter_hidden, grad_block)
    in_sum, up_sum = lax.psum((in_term, up_term), "fsdp")

    gradient_planes = jnp.stack(
        [prescale_gradient[:, i * plane_columns : (i + 1) * plane_columns] for i in range(depth)]
    )
    gradient_at = [
        lax.dynamic_index_in_dim(gradient_planes, plane_of[p], 0, keepdims=False)
        for p in range(depth)
    ]

    product = [0.0] * depth
    cross = [0.0] * depth
    gradient_parts = []
    for (low, high), blocks in zip(cuts, gathered):
        rows = attention_output[:, low:high]
        down_rows = adapter_down[low:high]
        running = nt(lowrank_gradient, down_rows)
        for p in range(depth):
            product[p] = product[p] + nt(rows, blocks[p])
            cross[p] = cross[p] + lax.dot_general(
                down_rows, blocks[p], (((0,), (1,)), ((), ())), preferred_element_type=jnp.float32
            )
            running = running + nn(gradient_at[p], blocks[p])
        gradient_parts.append(running.astype(jnp.bfloat16))
    input_gradient = jnp.concatenate(gradient_parts, axis=1)

    def to_blocks(parts):
        stacked = jnp.stack(parts)

        def of_block(index):
            return [
                lax.dynamic_index_in_dim(
                    stacked, position_of[index * block_planes + i], 0, keepdims=False
                )
                for i in range(block_planes)
            ]

        def joined(index):
            return jnp.concatenate(of_block(index), axis=1)

        total = joined(tensor_index).astype(jnp.float32)
        for shift in range(1, tensor_count):
            target = (tensor_index + shift) % tensor_count
            received = lax.ppermute(
                joined(target), "tensor", [(i, (i + shift) % tensor_count) for i in range(tensor_count)]
            )
            total = total + received.astype(jnp.float32)
        return total

    base_block = to_blocks([part.astype(jnp.bfloat16) for part in product])
    pre_block = base_block + nn(adapter_hidden, own_block(adapter_up))
    layer_out = (pre_block * scale_block[None, :]).astype(jnp.bfloat16)
    weighted_sum = sum_over(jnp.sum(cotangent.astype(jnp.float32) * pre_block, axis=0), "fsdp")
    weighted_block = weighted_sum / norms_block
    coef_block = -weighted_block * magnitude_block / (norms_block * norms_block)
    column_coefficient = lax.all_gather(coef_block, "tensor", axis=0, tiled=True)

    scaled_up = (column_coefficient[:, None] * adapter_up.astype(jnp.float32).T).astype(jnp.bfloat16)
    up_inner = nn(adapter_up, scaled_up)
    scaled_planes = scaled_up.reshape(depth, plane_columns, rank)
    scaled_at = [
        lax.dynamic_index_in_dim(scaled_planes, plane_of[p], 0, keepdims=False)
        for p in range(depth)
    ]
    norm_parts = []
    for blocks in gathered:
        running = tn(blocks[0], scaled_at[0])
        for p in range(1, depth):
            running = running + tn(blocks[p], scaled_at[p])
        norm_parts.append(running)
    norm_down = jnp.concatenate(norm_parts, axis=0)
    down_gradient = (
        in_sum
        + norm_down
        + jnp.dot(adapter_down.astype(jnp.float32), up_inner, precision=lax.Precision.HIGHEST)
    ) * grad_scale

    gram = sum_over(tn(adapter_down, adapter_down), "tensor")
    project = to_blocks(cross) + jnp.dot(
        gram, own_block(adapter_up).astype(jnp.float32), precision=lax.Precision.HIGHEST
    )
    d_up = (up_sum + project * coef_block[None, :]) * grad_scale
    d_magnitude = weighted_block * grad_scale
    return (layer_out, input_gradient, down_gradient, d_up, d_magnitude)


def solution(mesh):
    return jax.shard_map(
        on_device,
        mesh=mesh,
        in_specs=(
            P("fsdp", "tensor"),
            P("tensor", "fsdp"),
            P("tensor", None),
            P(),
            P(),
            P("fsdp", "tensor"),
        ),
        out_specs=(
            P("fsdp", "tensor"),
            P("fsdp", "tensor"),
            P("tensor", None),
            P(None, "tensor"),
            P("tensor"),
        ),
        check_vma=False,
    )
```

time: 899 us -> 570 us (0.63)
  waiting for transfers between devices: 715 us -> 222 us
  starting transfers between devices: 0.38 us -> 65.6 us
  local copies, waits for them, and re-layouts: 1.24 us -> 43.4 us
  other arithmetic: 5.58 us -> 36.6 us
  between operations: 13.9 us -> 31.1 us
    all_gather x1 -> x0, waiting for transfers between devices: 688 us -> none  [on_device(): piece_columns = lax.all_gather(frozen_weight, 'fsdp', axis=1, tiled=True)]
    ppermute x0 -> x59, waiting for transfers between devices: none -> 222 us  [the longest x33 139 us: flip(): return lax.ppermute(value, axis, pairs)]
    ppermute x0 -> x59, starting transfers between devices: none -> 65.5 us  [the longest x33 30.5 us: flip(): return lax.ppermute(value, axis, pairs)]
    all_gather x0 -> x1, blocking collectives: none -> 44.8 us  [on_device(): square_sum = lax.all_gather(square_own, 'fsdp', axis=0, tiled=True)]
    psum x2 -> x0, blocking collectives: 44.6 us -> none  [the longest x1 40.7 us: on_device(): lax.psum((weighted_local, in_term, up_term), 'fsdp')]
    psum x1, waiting for transfers between devices: 25.9 us -> 0.02 us  [on_device(): in_sum, up_sum = lax.psum((in_term, up_term), 'fsdp')]
    unnamed x14 -> x181, local copies, waits for them, and re-layouts: 1.23 us -> 23.3 us
    another operation x0 -> x52, other arithmetic: none -> 19.3 us  [the longest x49 17.6 us: both(): return jnp.stack([low, high], axis=axis)]
  transfers between devices with their start and end apart: 5 -> 61, of which waited for: 2 -> 24; matrix products, arithmetic and copies ran while one was open for 13% -> 30% of each run, Pallas kernels for 0% -> 0%
where the time goes in v1:
time: 570 us; the launch traced here: 562 us
  waiting for transfers between devices  222 us (39%)
  matrix products  117 us (21%)
  starting transfers between devices  65.6 us (12%)
  blocking collectives  46.8 us (8%)
  local copies, waits for them, and re-layouts  43.4 us (8%)
  other arithmetic  36.6 us (6%)
  between operations  31.1 us (5%)
    ppermute x33, waiting for transfers between devices, flip(): return lax.ppermute(value, axis, pairs)  139 us
    ppermute x12, waiting for transfers between devices, along_z(): lax.ppermute(down, 'fsdp', [(i, i - 4) for i in range(4, count) if i // 4...  82.8 us
    dot_general x20, matrix products, nn(): return jnp.dot(a, b, preferred_element_type=jnp.float32)  45.7 us
    all_gather x1, blocking collectives, on_device(): square_sum = lax.all_gather(square_own, 'fsdp', axis=0, tiled=True)  44.8 us
    dot_general x21, matrix products, nt(): lax.dot_general(a, b, (((1,), (1,)), ((), ())), preferred_element_type=jn...  34.2 us
    ppermute x33, starting transfers between devices, flip(): return lax.ppermute(value, axis, pairs)  30.5 us
    unnamed x181, local copies, waits for them, and re-layouts  23.3 us
    ppermute x12, starting transfers between devices, along_z(): lax.ppermute(up, 'fsdp', [(i, i + 4) for i in range(count - 4) if i // 4...  19.2 us
  transfers between devices with their start and end apart: 61, of which 24 were waited for; matrix products, arithmetic and copies ran while one was open for 30% of the time, Pallas kernels for 0%

profile of v1, /device:TPU:0, one launch (start us, length us, event | category | flops | bytes accessed | tf_op | source)
XLA Modules:
  0.0 562.1 jit_solution(13259129270615099813)
XLA Ops:
  7.2 2.9 copy.42
  11.3 2.9 collective-permute-start.4
  14.3 4.3 collective-permute-start.14
  21.6 3.6 fusion.173
  44.5 44.8 %all-gather = f32[16,1,256]{2,1,0:T(1,128)S(1)} all-gather(f32[1,1,256]{2,1,0:T(1,128)S(1)} %bitcast.430), channel_id=1, replica_groups=mesh['fsdp'=16,'tensor'=2] {'fsdp'}, dimensions={0}, use_global_device_ids=true | all-gather | bytes 17408 | tf_op jit(solution)/shard_map/all_gather | solution.py:125
  92.5 2.3 collective-permute-start
  95.3 12.2 %collective-permute-done = bf16[256,1024]{1,0:T(8,128)(2,1)S(1)} collective-permute-done((bf16[256,1024]{1,0:T(8,128)(2,1)S(1)}, bf16[256,1024]{1,0:T(8,128)(2,1)S(1)}, u32[]{:S(2)}, u32[]{:S(2)}) %collective-permute-start) | collective-permute-done | bytes 524320 | tf_op jit(solution)/shard_map/ppermute | solution.py:12
  113.0 17.0 %collective-permute-done.3 = bf16[2,256,1024]{2,1,0:T(8,128)(2,1)S(1)} collective-permute-done((bf16[2,256,1024]{2,1,0:T(8,128)(2,1)S(1)}, bf16[2,256,1024]{2,1,0:T(8,128)(2,1)S(1)}, u32[]{:S(2)}, u32[]{:S(2)}) %collective-permute-start.3) | collective-permute-done | bytes 1048608 | tf_op jit(solution)/shard_map/ppermute | solution.py:12
  132.0 4.6 collective-permute-start.11
  137.3 8.1 %collective-permute-done.29 = bf16[256,1024]{1,0:T(8,128)(2,1)S(1)} collective-permute-done((bf16[256,1024]{1,0:T(8,128)(2,1)S(1)}, bf16[256,1024]{1,0:T(8,128)(2,1)S(1)}, u32[]{:S(2)}, u32[]{:S(2)}) %collective-permute-start.29) | collective-permute-done | bytes 524320 | tf_op jit(solution)/shard_map/ppermute | solution.py:43
  147.5 4.9 collective-permute-done.7
  155.6 6.6 %collective-permute-done.33 = bf16[256,1024]{1,0:T(8,128)(2,1)S(1)} collective-permute-done((bf16[256,1024]{1,0:T(8,128)(2,1)S(1)}, bf16[256,1024]{1,0:T(8,128)(2,1)S(1)}, u32[]{:S(2)}, u32[]{:S(2)}) %collective-permute-start.33) | collective-permute-done | bytes 524320 | tf_op jit(solution)/shard_map/ppermute | solution.py:43
  162.9 8.3 %collective-permute-done.43 = bf16[256,1024]{1,0:T(8,128)(2,1)S(1)} collective-permute-done((bf16[256,1024]{1,0:T(8,128)(2,1)S(1)}, bf16[256,1024]{1,0:T(8,128)(2,1)S(1)}, u32[]{:S(2)}, u32[]{:S(2)}) %collective-permute-start.43) | collective-permute-done | bytes 524320 | tf_op jit(solution)/shard_map/ppermute | solution.py:43
  177.3 28.0 %collective-permute-done.47 = bf16[256,1024]{1,0:T(8,128)(2,1)S(1)} collective-permute-done((bf16[256,1024]{1,0:T(8,128)(2,1)S(1)}, bf16[256,1024]{1,0:T(8,128)(2,1)S(1)}, u32[]{:S(2)}, u32[]{:S(2)}) %collective-permute-start.47) | collective-permute-done | bytes 524320 | tf_op jit(solution)/shard_map/ppermute | solution.py:43
  208.7 9.0 %collective-permute-done.20 = bf16[256,1024]{1,0:T(8,128)(2,1)S(1)} collective-permute-done((bf16[256,1024]{1,0:T(8,128)(2,1)S(1)}, bf16[256,1024]{1,0:T(8,128)(2,1)S(1)}, u32[]{:S(2)}, u32[]{:S(2)}) %collective-permute-start.20) | collective-permute-done | bytes 524320 | tf_op jit(solution)/shard_map/ppermute | solution.py:12
  222.9 9.6 %collective-permute-done.34 = bf16[256,1024]{1,0:T(8,128)(2,1)S(1)} collective-permute-done((bf16[256,1024]{1,0:T(8,128)(2,1)S(1)}, bf16[256,1024]{1,0:T(8,128)(2,1)S(1)}, u32[]{:S(2)}, u32[]{:S(2)}) %collective-permute-start.34) | collective-permute-done | bytes 524320 | tf_op jit(solution)/shard_map/ppermute | solution.py:12
  234.8 5.3 collective-permute-done.48
  246.0 2.3 fusion.10
  249.9 8.8 %collective-permute-done.21 = bf16[2,256,1024]{2,1,0:T(8,128)(2,1)S(1)} collective-permute-done((bf16[2,256,1024]{2,1,0:T(8,128)(2,1)S(1)}, bf16[2,256,1024]{2,1,0:T(8,128)(2,1)S(1)}, u32[]{:S(2)}, u32[]{:S(2)}) %collective-permute-start.21) | collective-permute-done | bytes 1048608 | tf_op jit(solution)/shard_map/ppermute | solution.py:12
  260.0 21.2 %collective-permute-done.35 = bf16[2,256,1024]{2,1,0:T(8,128)(2,1)S(1)} collective-permute-done((bf16[2,256,1024]{2,1,0:T(8,128)(2,1)S(1)}, bf16[2,256,1024]{2,1,0:T(8,128)(2,1)S(1)}, u32[]{:S(2)}, u32[]{:S(2)}) %collective-permute-start.35) | collective-permute-done | bytes 1048608 | tf_op jit(solution)/shard_map/ppermute | solution.py:12
  281.4 16.5 %collective-permute-done.49 = bf16[2,256,1024]{2,1,0:T(8,128)(2,1)S(1)} collective-permute-done((bf16[2,256,1024]{2,1,0:T(8,128)(2,1)S(1)}, bf16[2,256,1024]{2,1,0:T(8,128)(2,1)S(1)}, u32[]{:S(2)}, u32[]{:S(2)}) %collective-permute-start.49) | collective-permute-done | bytes 1048608 | tf_op jit(solution)/shard_map/ppermute | solution.py:12
  305.0 19.0 %collective-permute-done.31 = bf16[2,256,1024]{2,1,0:T(8,128)(2,1)S(1)} collective-permute-done((bf16[2,256,1024]{2,1,0:T(8,128)(2,1)S(1)}, bf16[2,256,1024]{2,1,0:T(8,128)(2,1)S(1)}, u32[]{:S(2)}, u32[]{:S(2)}) %collective-permute-start.31) | collective-permute-done | bytes 1048608 | tf_op jit(solution)/shard_map/ppermute | solution.py:12
  331.6 20.5 %collective-permute-done.23 = bf16[2,256,1024]{2,1,0:T(8,128)(2,1)} collective-permute-done((bf16[2,256,1024]{2,1,0:T(8,128)(2,1)S(1)}, bf16[2,256,1024]{2,1,0:T(8,128)(2,1)}, u32[]{:S(2)}, u32[]{:S(2)}) %collective-permute-start.23) | collective-permute-done | bytes 1048608 | tf_op jit(solution)/shard_map/ppermute | solution.py:43
  355.5 2.7 fusion.54
  358.2 2.6 fusion.52
  360.8 2.6 fusion.50
  363.4 11.1 %collective-permute-done.40 = bf16[2,256,1024]{2,1,0:T(8,128)(2,1)S(1)} collective-permute-done((bf16[2,256,1024]{2,1,0:T(8,128)(2,1)S(1)}, bf16[2,256,1024]{2,1,0:T(8,128)(2,1)S(1)}, u32[]{:S(2)}, u32[]{:S(2)}) %collective-permute-start.40) | collective-permute-done | bytes 1048608 | tf_op jit(solution)/shard_map/ppermute | solution.py:43
  378.4 3.0 multiply_convert_fusion
  384.9 2.6 fusion.46
  388.0 2.7 fusion.44
  392.7 2.6 fusion.42
  395.3 2.6 fusion.40
  400.3 4.3 select_select_fusion.3
  406.4 2.6 fusion.32
  409.0 2.6 fusion.34
  411.6 2.6 fusion.24
  414.2 2.6 fusion.26
  416.9 6.6 %add_convert_fusion.1 = bf16[512,1024]{1,0:T(8,128)(2,1)} fusion(f32[512,1024]{1,0:T(8,128)} %fusion.26, f32[512,1024]{1,0:T(8,128)} %fusion.34, f32[512,1024]{1,0:T(8,128)} %fusion.132, f32[512,1024]{1,0:T(8,128)} %fusion.42, bf16[1024,1024]{1,0:T(8,128)(2,1)S(1)} %bitcast.357, bf16[4,512,1024]{2,1,0:T(8,128)(2,1)} %copy-done.46, s32[]{:T(128)S(6)} %select_n.554), kind=kOutput, calls=%fused_computation.36 | convolution fusion | flops 1076363264 | bytes 12582916 | tf_op jit(solution)/shard_map/dot_general | solution.py:86
  465.2 6.9 %collective-permute-done.38 = bf16[2,256,1024]{2,1,0:T(8,128)(2,1)S(1)} collective-permute-done((bf16[2,256,1024]{2,1,0:T(8,128)(2,1)S(1)}, bf16[2,256,1024]{2,1,0:T(8,128)(2,1)S(1)}, u32[]{:S(2)}, u32[]{:S(2)}) %collective-permute-start.38) | collective-permute-done | bytes 1048608 | tf_op jit(solution)/shard_map/ppermute | solution.py:12
  487.2 3.1 pad_maximum_fusion.19
  492.5 2.6 copy.52
  495.2 2.5 fusion.16
  497.7 2.4 fusion.15
  507.7 4.4 fusion.4
  520.9 2.4 collective-permute-done.55
  525.6 2.5 collective-permute-done.56
  549.8 2.9 fusion.3
  552.7 2.3 fusion.97
  (428 shorter events, 182.1 us)
Async XLA Ops:
  7.2 371.3 %all-gather.3.cloned.1.call-start = ((), (), s32[]{:S(2)}) async-start(), calls=%async_computation | async-start | bytes 6291456 | tf_op jit(solution)/shard_map/all_gather | solution.py:131
  11.3 78.1 %collective-permute-start.4 = (bf16[256,1024]{1,0:T(8,128)(2,1)}, bf16[256,1024]{1,0:T(8,128)(2,1)}, u32[]{:S(2)}, u32[]{:S(2)}) collective-permute-start(bf16[256,1024]{1,0:T(8,128)(2,1)} %get-tuple-element.62), channel_id=1, source_target_pairs={{0,2},{2,0},{4,6},{6,4},{8,10},{10,8},{12,14},{14,12},{16,18},{18,... | collective-permute-start | bytes 1572872 | tf_op jit(solution)/shard_map/ppermute | solution.py:12
  14.3 81.0 %collective-permute-start.14 = (bf16[256,1024]{1,0:T(8,128)(2,1)}, bf16[256,1024]{1,0:T(8,128)(2,1)}, u32[]{:S(2)}, u32[]{:S(2)}) collective-permute-start(bf16[256,1024]{1,0:T(8,128)(2,1)} %get-tuple-element.62), channel_id=1, source_target_pairs={{0,8},{2,10},{4,12},{6,14},{8,16},{10,18},{12,20},{14,22},{16,24},... | collective-permute-start | bytes 1572872 | tf_op jit(solution)/shard_map/ppermute | solution.py:42
  18.6 72.2 %collective-permute-start.6 = (bf16[256,1024]{1,0:T(8,128)(2,1)}, bf16[256,1024]{1,0:T(8,128)(2,1)}, u32[]{:S(2)}, u32[]{:S(2)}) collective-permute-start(bf16[256,1024]{1,0:T(8,128)(2,1)} %get-tuple-element.61), channel_id=1, source_target_pairs={{0,4},{2,6},{4,0},{6,2},{8,12},{10,14},{12,8},{14,10},{16,20},{18,... | collective-permute-start | bytes 1572872 | tf_op jit(solution)/shard_map/ppermute | solution.py:12
  20.1 70.8 %collective-permute-start.2 = (bf16[256,1024]{1,0:T(8,128)(2,1)}, bf16[256,1024]{1,0:T(8,128)(2,1)}, u32[]{:S(2)}, u32[]{:S(2)}) collective-permute-start(bf16[256,1024]{1,0:T(8,128)(2,1)} %get-tuple-element.60), channel_id=1, source_target_pairs={{0,4},{2,6},{4,0},{6,2},{8,12},{10,14},{12,8},{14,10},{16,20},{18,... | collective-permute-start | bytes 1572872 | tf_op jit(solution)/shard_map/ppermute | solution.py:12
  21.4 21.8 %collective-permute-start.52 = (f32[256]{0:T(256)S(1)}, f32[256]{0:T(256)S(1)}, u32[]{:S(2)}, u32[]{:S(2)}) collective-permute-start(f32[256]{0:T(256)S(1)} %fusion.9), channel_id=1, source_target_pairs={{0,1},{1,0},{2,3},{3,2},{4,5},{5,4},{6,7},{7,6},{8,9},{9,8},{10,11... | collective-permute-start | bytes 3080 | tf_op jit(solution)/shard_map/ppermute | solution.py:12
  21.5 528.2 %all-reduce.3.cloned.1.call-start = ((), (), s32[]{:S(2)}) async-start(), calls=%async_computation.1 | async-start | bytes 3145728 | tf_op jit(solution)/shard_map/psum | solution.py:145
  43.2 67.8 %collective-permute-start.15 = (bf16[256,1024]{1,0:T(8,128)(2,1)}, bf16[256,1024]{1,0:T(8,128)(2,1)S(1)}, u32[]{:S(2)}, u32[]{:S(2)}) collective-permute-start(bf16[256,1024]{1,0:T(8,128)(2,1)} %get-tuple-element.62), channel_id=1, source_target_pairs={{8,0},{10,2},{12,4},{14,6},{16,8},{18,10},{20,12},{22,14},{24,16},... | collective-permute-start | bytes 1572872 | tf_op jit(solution)/shard_map/ppermute | solution.py:43
  89.4 22.9 %collective-permute-start.18 = (bf16[256,1024]{1,0:T(8,128)(2,1)}, bf16[256,1024]{1,0:T(8,128)(2,1)S(1)}, u32[]{:S(2)}, u32[]{:S(2)}) collective-permute-start(bf16[256,1024]{1,0:T(8,128)(2,1)} %get-tuple-element.61), channel_id=1, source_target_pairs={{0,8},{2,10},{4,12},{6,14},{8,16},{10,18},{12,20},{14,22},{16,24},... | collective-permute-start | bytes 1572872 | tf_op jit(solution)/shard_map/ppermute | solution.py:42
  94.9 35.1 %collective-permute-start.3 = (bf16[2,256,1024]{2,1,0:T(8,128)(2,1)S(1)}, bf16[2,256,1024]{2,1,0:T(8,128)(2,1)S(1)}, u32[]{:S(2)}, u32[]{:S(2)}) collective-permute-start(bf16[2,256,1024]{2,1,0:T(8,128)(2,1)S(1)} %pad_maximum_fusion.21), channel_id=1, source_target_pairs={{0,2},{2,0},{4,6},{6,4},{8,10},{10,8},{12,14},{14,12},{16,18},{18,... | collective-permute-start | bytes 3145736 | tf_op jit(solution)/shard_map/ppermute | solution.py:12
  95.3 51.5 %collective-permute-start.5 = (bf16[2,256,1024]{2,1,0:T(8,128)(2,1)S(1)}, bf16[2,256,1024]{2,1,0:T(8,128)(2,1)S(1)}, u32[]{:S(2)}, u32[]{:S(2)}) collective-permute-start(bf16[2,256,1024]{2,1,0:T(8,128)(2,1)S(1)} %pad_maximum_fusion.22), channel_id=1, source_target_pairs={{0,4},{2,6},{4,0},{6,2},{8,12},{10,14},{12,8},{14,10},{16,20},{18,... | collective-permute-start | bytes 3145736 | tf_op jit(solution)/shard_map/ppermute | solution.py:12
  107.6 44.7 %collective-permute-start.7 = (bf16[2,256,1024]{2,1,0:T(8,128)(2,1)S(1)}, bf16[2,256,1024]{2,1,0:T(8,128)(2,1)S(1)}, u32[]{:S(2)}, u32[]{:S(2)}) collective-permute-start(bf16[2,256,1024]{2,1,0:T(8,128)(2,1)S(1)} %pad_maximum_fusion.23), channel_id=1, source_target_pairs={{0,2},{2,0},{4,6},{6,4},{8,10},{10,8},{12,14},{14,12},{16,18},{18,... | collective-permute-start | bytes 3145736 | tf_op jit(solution)/shard_map/ppermute | solution.py:12
  111.0 21.0 %collective-permute-start.19 = (bf16[256,1024]{1,0:T(8,128)(2,1)}, bf16[256,1024]{1,0:T(8,128)(2,1)S(1)}, u32[]{:S(2)}, u32[]{:S(2)}) collective-permute-start(bf16[256,1024]{1,0:T(8,128)(2,1)} %get-tuple-element.61), channel_id=1, source_target_pairs={{8,0},{10,2},{12,4},{14,6},{16,8},{18,10},{20,12},{22,14},{24,16},... | collective-permute-start | bytes 1572872 | tf_op jit(solution)/shard_map/ppermute | solution.py:43
  112.3 24.3 %collective-permute-start.28 = (bf16[256,1024]{1,0:T(8,128)(2,1)}, bf16[256,1024]{1,0:T(8,128)(2,1)S(1)}, u32[]{:S(2)}, u32[]{:S(2)}) collective-permute-start(bf16[256,1024]{1,0:T(8,128)(2,1)} %collective-permute-done.14), channel_id=1, source_target_pairs={{8,16},{10,18},{12,20},{14,22},{16,24},{18,26},{20,28},{22,30},{9,... | collective-permute-start | bytes 1572872 | tf_op jit(solution)/shard_map/ppermute | solution.py:42
  132.0 116.4 %collective-permute-start.11 = (bf16[2,256,1024]{2,1,0:T(8,128)(2,1)S(1)}, bf16[2,256,1024]{2,1,0:T(8,128)(2,1)S(1)}, u32[]{:S(2)}, u32[]{:S(2)}) collective-permute-start(bf16[2,256,1024]{2,1,0:T(8,128)(2,1)S(1)} %pad_maximum_fusion.21), channel_id=1, source_target_pairs={{0,8},{2,10},{4,12},{6,14},{8,16},{10,18},{12,20},{14,22},{16,24},... | collective-permute-start | bytes 3145736 | tf_op jit(solution)/shard_map/ppermute | solution.py:42
  136.6 17.7 %collective-permute-start.32 = (bf16[256,1024]{1,0:T(8,128)(2,1)S(1)}, bf16[256,1024]{1,0:T(8,128)(2,1)S(1)}, u32[]{:S(2)}, u32[]{:S(2)}) collective-permute-start(bf16[256,1024]{1,0:T(8,128)(2,1)S(1)} %collective-permute-done.18), channel_id=1, source_target_pairs={{8,16},{10,18},{12,20},{14,22},{16,24},{18,26},{20,28},{22,30},{9,... | collective-permute-start | bytes 1572872 | tf_op jit(solution)/shard_map/ppermute | solution.py:42
  145.5 16.7 %collective-permute-start.33 = (bf16[256,1024]{1,0:T(8,128)(2,1)S(1)}, bf16[256,1024]{1,0:T(8,128)(2,1)S(1)}, u32[]{:S(2)}, u32[]{:S(2)}) collective-permute-start(bf16[256,1024]{1,0:T(8,128)(2,1)S(1)} %collective-permute-done.19), channel_id=1, source_target_pairs={{8,0},{10,2},{12,4},{14,6},{16,8},{18,10},{20,12},{22,14},{9,1},{1... | collective-permute-start | bytes 1572872 | tf_op jit(solution)/shard_map/ppermute | solution.py:43
  152.3 18.9 %collective-permute-start.43 = (bf16[256,1024]{1,0:T(8,128)(2,1)S(1)}, bf16[256,1024]{1,0:T(8,128)(2,1)S(1)}, u32[]{:S(2)}, u32[]{:S(2)}) collective-permute-start(bf16[256,1024]{1,0:T(8,128)(2,1)S(1)} %collective-permute-done.29), channel_id=1, source_target_pairs={{8,0},{10,2},{12,4},{14,6},{9,1},{11,3},{13,5},{15,7}} | collective-permute-start | bytes 1572872 | tf_op jit(solution)/shard_map/ppermute | solution.py:43
  154.3 146.5 %collective-permute-start.12 = (bf16[2,256,1024]{2,1,0:T(8,128)(2,1)S(1)}, bf16[2,256,1024]{2,1,0:T(8,128)(2,1)S(1)}, u32[]{:S(2)}, u32[]{:S(2)}) collective-permute-start(bf16[2,256,1024]{2,1,0:T(8,128)(2,1)S(1)} %pad_maximum_fusion.21), channel_id=1, source_target_pairs={{8,0},{10,2},{12,4},{14,6},{16,8},{18,10},{20,12},{22,14},{24,16},... | collective-permute-start | bytes 3145736 | tf_op jit(solution)/shard_map/ppermute | solution.py:43
  162.2 58.7 %collective-permute-start.1 = (bf16[2,256,1024]{2,1,0:T(8,128)(2,1)S(1)}, bf16[2,256,1024]{2,1,0:T(8,128)(2,1)S(1)}, u32[]{:S(2)}, u32[]{:S(2)}) collective-permute-start(bf16[2,256,1024]{2,1,0:T(8,128)(2,1)S(1)} %pad_maximum_fusion.20), channel_id=1, source_target_pairs={{0,4},{2,6},{4,0},{6,2},{8,12},{10,14},{12,8},{14,10},{16,20},{18,... | collective-permute-start | bytes 3145736 | tf_op jit(solution)/shard_map/ppermute | solution.py:12
  171.2 34.1 %collective-permute-start.47 = (bf16[256,1024]{1,0:T(8,128)(2,1)S(1)}, bf16[256,1024]{1,0:T(8,128)(2,1)S(1)}, u32[]{:S(2)}, u32[]{:S(2)}) collective-permute-start(bf16[256,1024]{1,0:T(8,128)(2,1)S(1)} %collective-permute-done.33), channel_id=1, source_target_pairs={{8,0},{10,2},{12,4},{14,6},{9,1},{11,3},{13,5},{15,7}} | collective-permute-start | bytes 1572872 | tf_op jit(solution)/shard_map/ppermute | solution.py:43
  176.2 31.2 %collective-permute-start.16 = (bf16[256,1024]{1,0:T(8,128)(2,1)S(1)}, bf16[256,1024]{1,0:T(8,128)(2,1)S(1)}, u32[]{:S(2)}, u32[]{:S(2)}) collective-permute-start(bf16[256,1024]{1,0:T(8,128)(2,1)S(1)} %get-tuple-element.95), channel_id=1, source_target_pairs={{0,2},{2,0},{4,6},{6,4},{8,10},{10,8},{12,14},{14,12},{16,18},{18,... | collective-permute-start | bytes 1572872 | tf_op jit(solution)/shard_map/ppermute | solution.py:12
  219.5 23.7 %collective-permute-start.44 = (bf16[256,1024]{1,0:T(8,128)(2,1)S(1)}, bf16[256,1024]{1,0:T(8,128)(2,1)S(1)}, u32[]{:S(2)}, u32[]{:S(2)}) collective-permute-start(bf16[256,1024]{1,0:T(8,128)(2,1)S(1)} %get-tuple-element.82), channel_id=1, source_target_pairs={{0,2},{2,0},{4,6},{6,4},{8,10},{10,8},{12,14},{14,12},{16,18},{18,... | collective-permute-start | bytes 1572872 | tf_op jit(solution)/shard_map/ppermute | solution.py:12
  220.9 19.2 %collective-permute-start.48 = (bf16[256,1024]{1,0:T(8,128)(2,1)S(1)}, bf16[256,1024]{1,0:T(8,128)(2,1)S(1)}, u32[]{:S(2)}, u32[]{:S(2)}) collective-permute-start(bf16[256,1024]{1,0:T(8,128)(2,1)S(1)} %get-tuple-element.86), channel_id=1, source_target_pairs={{0,4},{2,6},{4,0},{6,2},{8,12},{10,14},{12,8},{14,10},{16,20},{18,... | collective-permute-start | bytes 1572872 | tf_op jit(solution)/shard_map/ppermute | solution.py:12
  232.6 26.1 %collective-permute-start.21 = (bf16[2,256,1024]{2,1,0:T(8,128)(2,1)S(1)}, bf16[2,256,1024]{2,1,0:T(8,128)(2,1)S(1)}, u32[]{:S(2)}, u32[]{:S(2)}) collective-permute-start(bf16[2,256,1024]{2,1,0:T(8,128)(2,1)S(1)} %pad_maximum_fusion.25), channel_id=1, source_target_pairs={{0,2},{2,0},{4,6},{6,4},{8,10},{10,8},{12,14},{14,12},{16,18},{18,... | collective-permute-start | bytes 3145736 | tf_op jit(solution)/shard_map/ppermute | solution.py:12
  240.1 41.0 %collective-permute-start.35 = (bf16[2,256,1024]{2,1,0:T(8,128)(2,1)S(1)}, bf16[2,256,1024]{2,1,0:T(8,128)(2,1)S(1)}, u32[]{:S(2)}, u32[]{:S(2)}) collective-permute-start(bf16[2,256,1024]{2,1,0:T(8,128)(2,1)S(1)} %pad_maximum_fusion.27), channel_id=1, source_target_pairs={{0,2},{2,0},{4,6},{6,4},{8,10},{10,8},{12,14},{14,12},{16,18},{18,... | collective-permute-start | bytes 3145736 | tf_op jit(solution)/shard_map/ppermute | solution.py:12
  243.2 54.7 %collective-permute-start.49 = (bf16[2,256,1024]{2,1,0:T(8,128)(2,1)S(1)}, bf16[2,256,1024]{2,1,0:T(8,128)(2,1)S(1)}, u32[]{:S(2)}, u32[]{:S(2)}) collective-permute-start(bf16[2,256,1024]{2,1,0:T(8,128)(2,1)S(1)} %pad_maximum_fusion.29), channel_id=1, source_target_pairs={{0,2},{2,0},{4,6},{6,4},{8,10},{10,8},{12,14},{14,12},{16,18},{18,... | collective-permute-start | bytes 3145736 | tf_op jit(solution)/shard_map/ppermute | solution.py:12
  248.4 53.2 %collective-permute-start.8 = (bf16[2,256,1024]{2,1,0:T(8,128)(2,1)S(1)}, bf16[2,256,1024]{2,1,0:T(8,128)(2,1)S(1)}, u32[]{:S(2)}, u32[]{:S(2)}) collective-permute-start(bf16[2,256,1024]{2,1,0:T(8,128)(2,1)S(1)} %pad_maximum_fusion.20), channel_id=1, source_target_pairs={{0,8},{2,10},{4,12},{6,14},{8,16},{10,18},{12,20},{14,22},{16,24},... | collective-permute-start | bytes 3145736 | tf_op jit(solution)/shard_map/ppermute | solution.py:42
  258.7 44.2 %collective-permute-start.9 = (bf16[2,256,1024]{2,1,0:T(8,128)(2,1)S(1)}, bf16[2,256,1024]{2,1,0:T(8,128)(2,1)S(1)}, u32[]{:S(2)}, u32[]{:S(2)}) collective-permute-start(bf16[2,256,1024]{2,1,0:T(8,128)(2,1)S(1)} %pad_maximum_fusion.20), channel_id=1, source_target_pairs={{8,0},{10,2},{12,4},{14,6},{16,8},{18,10},{20,12},{22,14},{24,16},... | collective-permute-start | bytes 3145736 | tf_op jit(solution)/shard_map/ppermute | solution.py:43
  281.1 22.2 %collective-permute-start.17 = (bf16[2,256,1024]{2,1,0:T(8,128)(2,1)S(1)}, bf16[2,256,1024]{2,1,0:T(8,128)(2,1)S(1)}, u32[]{:S(2)}, u32[]{:S(2)}) collective-permute-start(bf16[2,256,1024]{2,1,0:T(8,128)(2,1)S(1)} %pad_maximum_fusion.24), channel_id=1, source_target_pairs={{0,4},{2,6},{4,0},{6,2},{8,12},{10,14},{12,8},{14,10},{16,20},{18,... | collective-permute-start | bytes 3145736 | tf_op jit(solution)/shard_map/ppermute | solution.py:12
  297.9 26.1 %collective-permute-start.31 = (bf16[2,256,1024]{2,1,0:T(8,128)(2,1)S(1)}, bf16[2,256,1024]{2,1,0:T(8,128)(2,1)S(1)}, u32[]{:S(2)}, u32[]{:S(2)}) collective-permute-start(bf16[2,256,1024]{2,1,0:T(8,128)(2,1)S(1)} %pad_maximum_fusion.26), channel_id=1, source_target_pairs={{0,4},{2,6},{4,0},{6,2},{8,12},{10,14},{12,8},{14,10},{16,20},{18,... | collective-permute-start | bytes 3145736 | tf_op jit(solution)/shard_map/ppermute | solution.py:12
  300.9 28.6 %collective-permute-start.25 = (bf16[2,256,1024]{2,1,0:T(8,128)(2,1)S(1)}, bf16[2,256,1024]{2,1,0:T(8,128)(2,1)S(1)}, u32[]{:S(2)}, u32[]{:S(2)}) collective-permute-start(bf16[2,256,1024]{2,1,0:T(8,128)(2,1)S(1)} %collective-permute-done.11), channel_id=1, source_target_pairs={{8,16},{10,18},{12,20},{14,22},{16,24},{18,26},{20,28},{22,30},{9,... | collective-permute-start | bytes 3145736 | tf_op jit(solution)/shard_map/ppermute | solution.py:42
  301.6 28.0 %collective-permute-start.26 = (bf16[2,256,1024]{2,1,0:T(8,128)(2,1)S(1)}, bf16[2,256,1024]{2,1,0:T(8,128)(2,1)S(1)}, u32[]{:S(2)}, u32[]{:S(2)}) collective-permute-start(bf16[2,256,1024]{2,1,0:T(8,128)(2,1)S(1)} %collective-permute-done.12), channel_id=1, source_target_pairs={{8,0},{10,2},{12,4},{14,6},{16,8},{18,10},{20,12},{22,14},{9,1},{1... | collective-permute-start | bytes 3145736 | tf_op jit(solution)/shard_map/ppermute | solution.py:43
  302.9 50.9 %collective-permute-start.45 = (bf16[2,256,1024]{2,1,0:T(8,128)(2,1)S(1)}, bf16[2,256,1024]{2,1,0:T(8,128)(2,1)S(1)}, u32[]{:S(2)}, u32[]{:S(2)}) collective-permute-start(bf16[2,256,1024]{2,1,0:T(8,128)(2,1)S(1)} %pad_maximum_fusion.28), channel_id=1, source_target_pairs={{0,4},{2,6},{4,0},{6,2},{8,12},{10,14},{12,8},{14,10},{16,20},{18,... | collective-permute-start | bytes 3145736 | tf_op jit(solution)/shard_map/ppermute | solution.py:12
  303.3 27.0 %collective-permute-start.22 = (bf16[2,256,1024]{2,1,0:T(8,128)(2,1)S(1)}, bf16[2,256,1024]{2,1,0:T(8,128)(2,1)}, u32[]{:S(2)}, u32[]{:S(2)}) collective-permute-start(bf16[2,256,1024]{2,1,0:T(8,128)(2,1)S(1)} %collective-permute-done.8), channel_id=1, source_target_pairs={{8,16},{10,18},{12,20},{14,22},{16,24},{18,26},{20,28},{22,30},{9,... | collective-permute-start | bytes 3145736 | tf_op jit(solution)/shard_map/ppermute | solution.py:42
  324.0 28.2 %collective-permute-start.23 = (bf16[2,256,1024]{2,1,0:T(8,128)(2,1)S(1)}, bf16[2,256,1024]{2,1,0:T(8,128)(2,1)}, u32[]{:S(2)}, u32[]{:S(2)}) collective-permute-start(bf16[2,256,1024]{2,1,0:T(8,128)(2,1)S(1)} %collective-permute-done.9), channel_id=1, source_target_pairs={{8,0},{10,2},{12,4},{14,6},{16,8},{18,10},{20,12},{22,14},{9,1},{1... | collective-permute-start | bytes 3145736 | tf_op jit(solution)/shard_map/ppermute | solution.py:43
  329.5 223.2 %collective-permute-start.58 = (f32[64,64]{1,0:T(8,128)}, f32[64,64]{1,0:T(8,128)}, u32[]{:S(2)}, u32[]{:S(2)}) collective-permute-start(f32[64,64]{1,0:T(8,128)} %fusion.174), channel_id=1, source_target_pairs={{0,1},{1,0},{2,3},{3,2},{4,5},{5,4},{6,7},{7,6},{8,9},{9,8},{10,11... | collective-permute-start | bytes 49160 | tf_op jit(solution)/shard_map/ppermute | solution.py:12
  329.6 33.8 %collective-permute-start.39 = (bf16[2,256,1024]{2,1,0:T(8,128)(2,1)S(1)}, bf16[2,256,1024]{2,1,0:T(8,128)(2,1)S(1)}, u32[]{:S(2)}, u32[]{:S(2)}) collective-permute-start(bf16[2,256,1024]{2,1,0:T(8,128)(2,1)S(1)} %collective-permute-done.25), channel_id=1, source_target_pairs={{16,24},{18,26},{20,28},{22,30},{17,25},{19,27},{21,29},{23,31}} | collective-permute-start | bytes 3145736 | tf_op jit(solution)/shard_map/ppermute | solution.py:42
  330.3 44.2 %collective-permute-start.40 = (bf16[2,256,1024]{2,1,0:T(8,128)(2,1)S(1)}, bf16[2,256,1024]{2,1,0:T(8,128)(2,1)S(1)}, u32[]{:S(2)}, u32[]{:S(2)}) collective-permute-start(bf16[2,256,1024]{2,1,0:T(8,128)(2,1)S(1)} %collective-permute-done.26), channel_id=1, source_target_pairs={{8,0},{10,2},{12,4},{14,6},{9,1},{11,3},{13,5},{15,7}} | collective-permute-start | bytes 3145736 | tf_op jit(solution)/shard_map/ppermute | solution.py:43
  352.2 47.6 %collective-permute-start.36 = (bf16[2,256,1024]{2,1,0:T(8,128)(2,1)}, bf16[2,256,1024]{2,1,0:T(8,128)(2,1)}, u32[]{:S(2)}, u32[]{:S(2)}) collective-permute-start(bf16[2,256,1024]{2,1,0:T(8,128)(2,1)} %collective-permute-done.22), channel_id=1, source_target_pairs={{16,24},{18,26},{20,28},{22,30},{17,25},{19,27},{21,29},{23,31}} | collective-permute-start | bytes 3145736 | tf_op jit(solution)/shard_map/ppermute | solution.py:42
  353.8 46.5 %collective-permute-start.37 = (bf16[2,256,1024]{2,1,0:T(8,128)(2,1)}, bf16[2,256,1024]{2,1,0:T(8,128)(2,1)}, u32[]{:S(2)}, u32[]{:S(2)}) collective-permute-start(bf16[2,256,1024]{2,1,0:T(8,128)(2,1)} %collective-permute-done.23), channel_id=1, source_target_pairs={{8,0},{10,2},{12,4},{14,6},{9,1},{11,3},{13,5},{15,7}} | collective-permute-start | bytes 3145736 | tf_op jit(solution)/shard_map/ppermute | solution.py:43
  376.4 53.6 %collective-permute-start.13 = (bf16[2,256,1024]{2,1,0:T(8,128)(2,1)}, bf16[2,256,1024]{2,1,0:T(8,128)(2,1)}, u32[]{:S(2)}, u32[]{:S(2)}) collective-permute-start(bf16[2,256,1024]{2,1,0:T(8,128)(2,1)} %get-tuple-element.73), channel_id=1, source_target_pairs={{0,2},{2,0},{4,6},{6,4},{8,10},{10,8},{12,14},{14,12},{16,18},{18,... | collective-permute-start | bytes 3145736 | tf_op jit(solution)/shard_map/ppermute | solution.py:12
  376.9 55.3 %collective-permute-start.27 = (bf16[2,256,1024]{2,1,0:T(8,128)(2,1)}, bf16[2,256,1024]{2,1,0:T(8,128)(2,1)}, u32[]{:S(2)}, u32[]{:S(2)}) collective-permute-start(bf16[2,256,1024]{2,1,0:T(8,128)(2,1)} %get-tuple-element.48), channel_id=1, source_target_pairs={{0,2},{2,0},{4,6},{6,4},{8,10},{10,8},{12,14},{14,12},{16,18},{18,... | collective-permute-start | bytes 3145736 | tf_op jit(solution)/shard_map/ppermute | solution.py:12
  399.8 45.3 %collective-permute-start.41 = (bf16[2,256,1024]{2,1,0:T(8,128)(2,1)}, bf16[2,256,1024]{2,1,0:T(8,128)(2,1)}, u32[]{:S(2)}, u32[]{:S(2)}) collective-permute-start(bf16[2,256,1024]{2,1,0:T(8,128)(2,1)} %get-tuple-element.49), channel_id=1, source_target_pairs={{0,2},{2,0},{4,6},{6,4},{8,10},{10,8},{12,14},{14,12},{16,18},{18,... | collective-permute-start | bytes 3145736 | tf_op jit(solution)/shard_map/ppermute | solution.py:12
  404.6 47.6 %collective-permute-start.10 = (bf16[2,256,1024]{2,1,0:T(8,128)(2,1)}, bf16[2,256,1024]{2,1,0:T(8,128)(2,1)}, u32[]{:S(2)}, u32[]{:S(2)}) collective-permute-start(bf16[2,256,1024]{2,1,0:T(8,128)(2,1)} %get-tuple-element.74), channel_id=1, source_target_pairs={{0,4},{2,6},{4,0},{6,2},{8,12},{10,14},{12,8},{14,10},{16,20},{18,... | collective-permute-start | bytes 3145736 | tf_op jit(solution)/shard_map/ppermute | solution.py:12
  430.0 28.2 %collective-permute-start.24 = (bf16[2,256,1024]{2,1,0:T(8,128)(2,1)S(1)}, bf16[2,256,1024]{2,1,0:T(8,128)(2,1)S(1)}, u32[]{:S(2)}, u32[]{:S(2)}) collective-permute-start(bf16[2,256,1024]{2,1,0:T(8,128)(2,1)S(1)} %copy-done.59), channel_id=1, source_target_pairs={{0,4},{2,6},{4,0},{6,2},{8,12},{10,14},{12,8},{14,10},{16,20},{18,... | collective-permute-start | bytes 3145736 | tf_op jit(solution)/shard_map/ppermute | solution.py:12
  433.6 38.4 %collective-permute-start.38 = (bf16[2,256,1024]{2,1,0:T(8,128)(2,1)S(1)}, bf16[2,256,1024]{2,1,0:T(8,128)(2,1)S(1)}, u32[]{:S(2)}, u32[]{:S(2)}) collective-permute-start(bf16[2,256,1024]{2,1,0:T(8,128)(2,1)S(1)} %copy-done.57), channel_id=1, source_target_pairs={{0,4},{2,6},{4,0},{6,2},{8,12},{10,14},{12,8},{14,10},{16,20},{18,... | collective-permute-start | bytes 3145736 | tf_op jit(solution)/shard_map/ppermute | solution.py:12
  518.4 34.3 %collective-permute-start.57 = (f32[64,2048]{1,0:T(8,128)}, f32[64,2048]{1,0:T(8,128)}, u32[]{:S(2)}, u32[]{:S(2)}) collective-permute-start(f32[64,2048]{1,0:T(8,128)} %pad_maximum_fusion.31), channel_id=1, source_target_pairs={{0,1},{1,0},{2,3},{3,2},{4,5},{5,4},{6,7},{7,6},{8,9},{9,8},{10,11... | collective-permute-start | bytes 1572872 | tf_op jit(solution)/shard_map/ppermute | solution.py:188
  (101 other events, 875.7 us)
Sparse Core Ops, SparseCore 0:
  21.7 12.3 all-gather.2
  417.0 118.2 all-reduce.2
